TPU v7x, 256 devices: a whole 4x4x8 slice. The times are simulated.
256 devices in a mesh: group: 32 (over z, x), member: 8 (over y, core).
Axes of the slice: x: 4, y: 4, z: 8, core: 2. Of those that a mesh axis runs over, the one named last changes fastest.
Arguments:
- node_latent: bfloat16 [131072, 128], P(('group', 'member')), may hold values from -6 to 6
- edge_latent: bfloat16 [786432, 128], P(('group', 'member')), may hold values from -6 to 6
- edge_src: int32 [786432], P(('group', 'member')), may hold values from 0 to 767
- edge_dst: int32 [786432], P(('group', 'member')), may hold values from 0 to 511
- edge_count: int32 [256], P(('group', 'member')), may hold values from 1536 to 3072, as said below
- halo_send: int32 [256, 2, 128], P(('group', 'member')), may hold values from 0 to 511
- halo_count: int32 [256, 2], P(('group', 'member')), may hold values from 64 to 128, as said below
- pool_index: int32 [131072], P(('group', 'member')), may hold values from 0 to 255, as said below
- coarse_src: int32 [49152], P('group'), may hold values from 0 to 511
- coarse_dst: int32 [49152], P('group'), may hold values from 0 to 255
- coarse_count: int32 [32], P('group'), may hold values from 768 to 1536, as said below
- coarse_send: int32 [32, 2, 128], P('group'), may hold values from 0 to 255
- coarse_halo_count: int32 [32, 2], P('group'), may hold values from 64 to 128, as said below
- w_edge_in: bfloat16 [384, 128], replicated, may hold values from -0.3125 to 0.3125
- w_node_in: bfloat16 [256, 128], replicated, may hold values from -0.375 to 0.375
- w_cedge_in: bfloat16 [256, 128], replicated, may hold values from -0.375 to 0.375
- w_cnode_in: bfloat16 [256, 128], replicated, may hold values from -0.375 to 0.375
- w_outs: bfloat16 [5, 128, 128], replicated, may hold values from -0.5 to 0.5
- cot_nodes: bfloat16 [131072, 128], P(('group', 'member')), may hold values from -24 to 24
- cot_edges: bfloat16 [786432, 128], P(('group', 'member')), may hold values from -6 to 6
Outputs:
- new_nodes: bfloat16 [131072, 128], P(('group', 'member'))
- new_edges: bfloat16 [786432, 128], P(('group', 'member'))
- grad_nodes: bfloat16 [131072, 128], P(('group', 'member'))
- grad_edges: bfloat16 [786432, 128], P(('group', 'member'))
- grad_edge_in: float32 [384, 128], replicated
- grad_node_in: float32 [256, 128], replicated
- grad_cedge_in: float32 [256, 128], replicated
- grad_cnode_in: float32 [256, 128], replicated
- grad_outs: float32 [5, 128, 128], replicated
Inputs may be any that keep to these rules, and one draw needn't show every extreme that they name: `edge_count`: in every draw some fine partition has all 3072 edge rows live. `halo_count`: in every draw some send list is full. `pool_index`: every coarse node of a coarse partition receives at least one fine node of that partition. `coarse_count`: in every draw some coarse partition has all 1536 edge rows live. `coarse_halo_count`: in every draw some coarse send list is full.
All inputs are finite; a program needn't handle non-finite values.
Results may differ from a plain program's by a relative error of at most 0.022.
Values may be sent and summed in bfloat16 or wider, within the bound.
No kernel may reach another device: no remote copies, remote signals or barrier semaphores. Data moves between devices by JAX's collectives and lax.ppermute only.
A program may use at most 64 MiB of HBM per device.

v0:
```python
import jax
import jax.numpy as jnp
from jax import lax
from jax.sharding import PartitionSpec as P

POOL_RATIO = 16


eps = 1e-05


def with_halo(cells, sides, width):
    for axis, dim in sides:
        count = lax.axis_size(axis)
        ends = count - 1
        head = lax.slice_in_dim(cells, 0, width, axis=dim)
        tail = lax.slice_in_dim(cells, cells.shape[dim] - width, cells.shape[dim], axis=dim)
        cells = jnp.concatenate(
            [
                lax.ppermute(tail, axis, [(i, (i + 1) % count) for i in range(ends)]),
                cells,
                lax.ppermute(head, axis, [((i + 1) % count, i) for i in range(ends)]),
            ],
            axis=dim,
        )
    return cells


def widen(values):
    return lax.optimization_barrier(values).astype(jnp.float32)


def rounded(values):
    return widen(values.astype(jnp.bfloat16))


def segment_total(values, indices, row_count):
    return jax.ops.segment_sum(values, indices, num_segments=row_count)


def silu_slope(pre_act):
    sigmoid = jax.nn.sigmoid(pre_act)
    return sigmoid * (1.0 + pre_act * (1.0 - sigmoid))


def mlp_forward(inputs, w_first, w_second):
    pre_act = jnp.dot(inputs, w_first, preferred_element_type=jnp.float32)
    hidden = (pre_act * jax.nn.sigmoid(pre_act)).astype(jnp.bfloat16)
    outcome = jnp.dot(hidden, w_second, preferred_element_type=jnp.float32)
    centred = outcome - jnp.mean(outcome, axis=-1, keepdims=True)
    inv_scale = lax.rsqrt(jnp.mean(centred * centred, axis=-1, keepdims=True) + eps)
    normed = centred * inv_scale
    return (normed, (pre_act, hidden, normed, inv_scale))


def mlp_backward(grad_out, inputs, w_first, w_second, stored):
    pre_act, hidden, normed, inv_scale = stored
    grad_raw = inv_scale * (
        grad_out
        - jnp.mean(grad_out, axis=-1, keepdims=True)
        - normed * jnp.mean(grad_out * normed, axis=-1, keepdims=True)
    )
    grad_raw = grad_raw.astype(jnp.bfloat16)
    grad_second = jnp.dot(hidden.T, grad_raw, preferred_element_type=jnp.float32)
    grad_hidden = jnp.dot(grad_raw, w_second.T, preferred_element_type=jnp.float32)
    grad_pre = (grad_hidden * silu_slope(pre_act)).astype(jnp.bfloat16)
    grad_first = jnp.dot(inputs.T, grad_pre, preferred_element_type=jnp.float32)
    grad_inputs = jnp.dot(grad_pre, w_first.T, preferred_element_type=jnp.float32)
    return (grad_inputs, grad_first, grad_second)


def pick_rows(source_rows, send_rows, live_count):
    slot_mask = (jnp.arange(send_rows.shape[-1])[None, :] < live_count[:, None]).astype(
        source_rows.dtype
    )
    picked = source_rows[send_rows] * slot_mask[:, :, None]
    return picked.reshape(2 * send_rows.shape[-1], source_rows.shape[1])


def slot_returns(returned, send_rows, live_count, row_count):
    slot_width = send_rows.shape[-1]
    slot_mask = (jnp.arange(slot_width)[None, :] < live_count[:, None]).astype(jnp.float32)
    return segment_total(
        returned * slot_mask.reshape(2 * slot_width, 1),
        send_rows.reshape(2 * slot_width),
        row_count,
    )


def fine_extend(node_rows, send_rows, live_count):
    slot_width = send_rows.shape[-1]
    sent = pick_rows(node_rows, send_rows, live_count)
    padded = with_halo(sent, ((("group", "member"), 0),), slot_width)
    return jnp.concatenate([node_rows, padded[:slot_width], padded[3 * slot_width :]], 0)


def fine_return(grad_ext, send_rows, live_count, row_count):
    slot_width = send_rows.shape[-1]
    padded = with_halo(grad_ext[row_count:], ((("group", "member"), 0),), slot_width)
    returned = jnp.concatenate([padded[:slot_width], padded[3 * slot_width :]], 0)
    return slot_returns(returned, send_rows, live_count, row_count)


def coarse_extend(latents, send_rows, live_count):
    slot_width = send_rows.shape[-1]
    sent = pick_rows(latents, send_rows, live_count)
    padded = with_halo(sent, (("group", 0),), slot_width)
    return jnp.concatenate([latents, padded[:slot_width], padded[3 * slot_width :]], 0)


def coarse_return(grad_ext, send_rows, live_count, row_count):
    slot_width = send_rows.shape[-1]
    padded = with_halo(grad_ext[row_count:], (("group", 0),), slot_width)
    returned = jnp.concatenate([padded[:slot_width], padded[3 * slot_width :]], 0)
    return slot_returns(returned, send_rows, live_count, row_count)


def edge_section(extended, node_rows, edge_rows, sources, targets, live_count, w_first, w_second):
    inputs = jnp.concatenate([edge_rows, extended[sources], node_rows[targets]], 1)
    message, stored = mlp_forward(inputs, w_first, w_second)
    valid_rows = (jnp.arange(edge_rows.shape[0]) < live_count).astype(jnp.float32)[:, None]
    new_rows = (edge_rows.astype(jnp.float32) + valid_rows * message).astype(jnp.bfloat16)
    aggregate = segment_total(widen(new_rows) * valid_rows, targets, node_rows.shape[0]).astype(
        jnp.bfloat16
    )
    return (inputs, stored, valid_rows, new_rows, aggregate)


def coarse_section(extended, latents, sources, targets, valid_rows, w_first, w_second, row_count):
    inputs = jnp.concatenate([extended[sources], latents[targets]], 1)
    message, stored = mlp_forward(inputs, w_first, w_second)
    partial_value = segment_total(message * valid_rows, targets, row_count)
    return (inputs, stored, partial_value)


def on_device(
    node_latent,
    edge_latent,
    edge_src,
    edge_dst,
    edge_count,
    halo_send,
    halo_count,
    pool_index,
    coarse_src,
    coarse_dst,
    coarse_count,
    coarse_send,
    coarse_halo_count,
    w_edge_in,
    w_node_in,
    w_cedge_in,
    w_cnode_in,
    w_outs,
    cot_nodes,
    cot_edges,
):
    node_count = node_latent.shape[0]
    feat_width = node_latent.shape[1]
    members = lax.axis_size("member")
    coarse_rows = node_count * members // POOL_RATIO
    extended = fine_extend(node_latent, halo_send[0], halo_count[0])
    inputs, stored, valid_rows, new_edges, aggregate = edge_section(
        extended, node_latent, edge_latent, edge_src, edge_dst, edge_count[0], w_edge_in, w_outs[0]
    )
    node_in = jnp.concatenate([node_latent, aggregate], 1)
    update, stored_node = mlp_forward(node_in, w_node_in, w_outs[1])
    refined = (node_latent.astype(jnp.float32) + update).astype(jnp.bfloat16)
    refined_wide = widen(refined)
    local_sums = segment_total(refined_wide, pool_index, coarse_rows)
    local_counts = segment_total(jnp.ones((node_count,), jnp.float32), pool_index, coarse_rows)
    pooled_sums, divisor = lax.psum((local_sums, local_counts), "member")
    own_latents = (pooled_sums / divisor[:, None]).astype(jnp.bfloat16)
    coarse_ext = coarse_extend(own_latents, coarse_send[0], coarse_halo_count[0])
    coarse_valid = (jnp.arange(coarse_src.shape[0]) < coarse_count[0]).astype(jnp.float32)[:, None]
    coarse_in, stored_coarse, partial_value = coarse_section(
        coarse_ext,
        own_latents,
        coarse_src,
        coarse_dst,
        coarse_valid,
        w_cedge_in,
        w_outs[2],
        coarse_rows,
    )
    coarse_agg = partial_value.astype(jnp.bfloat16)
    coarse_node_in = jnp.concatenate([own_latents, coarse_agg], 1)
    coarse_update, stored_cnode = mlp_forward(coarse_node_in, w_cnode_in, w_outs[3])
    own_coarse = (own_latents.astype(jnp.float32) + coarse_update).astype(jnp.bfloat16)
    lifted = own_coarse[pool_index]
    new_nodes = (
        refined_wide + jnp.dot(lifted, w_outs[4], preferred_element_type=jnp.float32)
    ).astype(jnp.bfloat16)
    grad_lift_w = jnp.dot(lifted.T, cot_nodes, preferred_element_type=jnp.float32)
    grad_lifted = jnp.dot(cot_nodes, w_outs[4].T, preferred_element_type=jnp.float32)
    lifted_sums = segment_total(grad_lifted, pool_index, coarse_rows)
    grad_coarse = rounded(lax.psum(lifted_sums, "member"))
    grad_cnode_x, grad_cnode_first, grad_cnode_second = mlp_backward(
        grad_coarse, coarse_node_in, w_cnode_in, w_outs[3], stored_cnode
    )
    grad_own = grad_coarse + grad_cnode_x[:, :feat_width]
    grad_agg_own = grad_cnode_x[:, feat_width:].astype(jnp.bfloat16)
    grad_agg = widen(grad_agg_own)
    grad_message = grad_agg[coarse_dst] * coarse_valid
    grad_cin, grad_cedge_first, grad_cedge_second = mlp_backward(
        grad_message, coarse_in, w_cedge_in, w_outs[2], stored_coarse
    )
    grad_cext = segment_total(grad_cin[:, :feat_width], coarse_src, coarse_ext.shape[0])
    grad_from_edges = (
        segment_total(grad_cin[:, feat_width:], coarse_dst, coarse_rows)
        + grad_cext[:coarse_rows]
        + coarse_return(grad_cext, coarse_send[0], coarse_halo_count[0], coarse_rows)
    )
    grad_pool = rounded(grad_own + grad_from_edges) / divisor[:, None]
    grad_refined = rounded(cot_nodes.astype(jnp.float32) + grad_pool[pool_index])
    grad_node_x, grad_node_first, grad_node_second = mlp_backward(
        grad_refined, node_in, w_node_in, w_outs[1], stored_node
    )
    grad_aggregate = rounded(grad_node_x[:, feat_width:])
    grad_new = rounded(cot_edges.astype(jnp.float32) + valid_rows * grad_aggregate[edge_dst])
    grad_inputs, grad_edge_first, grad_edge_second = mlp_backward(
        grad_new * valid_rows, inputs, w_edge_in, w_outs[0], stored
    )
    grad_edges = (grad_new + grad_inputs[:, :feat_width]).astype(jnp.bfloat16)
    grad_ext = segment_total(
        grad_inputs[:, feat_width : 2 * feat_width], edge_src, extended.shape[0]
    )
    grad_total = (
        grad_refined
        + grad_node_x[:, :feat_width]
        + segment_total(grad_inputs[:, 2 * feat_width :], edge_dst, node_count)
        + grad_ext[:node_count]
        + fine_return(grad_ext, halo_send[0], halo_count[0], node_count)
    )
    fine_sums = lax.psum(
        (grad_edge_first, grad_edge_second, grad_node_first, grad_node_second, grad_lift_w),
        ("group", "member"),
    )
    coarse_sums = lax.psum(
        (grad_cedge_first, grad_cedge_second, grad_cnode_first, grad_cnode_second), "group"
    )
    summed = fine_sums + coarse_sums
    grad_outs = jnp.stack([summed[1], summed[3], summed[6], summed[8], summed[4]])
    return (
        new_nodes,
        new_edges,
        grad_total.astype(jnp.bfloat16),
        grad_edges,
        summed[0],
        summed[2],
        summed[5],
        summed[7],
        grad_outs,
    )


def solution(mesh):
    in_specs = (
        P(("group", "member"), None),
        P(("group", "member"), None),
        P(("group", "member")),
        P(("group", "member")),
        P(("group", "member")),
        P(("group", "member"), None, None),
        P(("group", "member"), None),
        P(("group", "member")),
        P("group"),
        P("group"),
        P("group"),
        P("group", None, None),
        P("group", None),
        P(),
        P(),
        P(),
        P(),
        P(),
        P(("group", "member"), None),
        P(("group", "member"), None),
    )
    out_specs = (
        P(("group", "member"), None),
        P(("group", "member"), None),
        P(("group", "member"), None),
        P(("group", "member"), None),
        P(),
        P(),
        P(),
        P(),
        P(),
    )
    return jax.shard_map(
        on_device, mesh=mesh, in_specs=in_specs, out_specs=out_specs, check_vma=False
    )
```

profile of v0, /device:TPU:1, one launch (start us, length us, event | category | flops | bytes accessed | tf_op | source)
XLA Modules:
  0.0 721.2 jit_solution(8231901173166402572)
XLA Ops:
  7.3 1.3 convert_bitcast_fusion
  9.3 1.6 gather_fusion
  11.1 4.6 collective-permute-start
  15.7 2.1 collective-permute-start.1
  17.8 1.3 constant_dynamic-update-slice_fusion.2
  22.8 1.7 fusion.57
  25.0 2.3 copy.56
  27.4 11.4 %gather_fusion.2 = bf16[3072,128]{1,0:T(8,128)(2,1)} fusion(bf16[512,128]{1,0:T(8,128)(2,1)S(1)} %copy-done.1, s32[3072]{0:T(1024)S(1)} %get-tuple-element.73), kind=kCustom, calls=%fused_computation.2 | custom fusion | bytes 1585152 | tf_op jit(solution)/shard_map/gather | solution.py:119
  38.9 2.7 scatter_custom_fusion.4
  41.6 4.1 scatter_custom_fusion.2
  45.7 24.7 %all-reduce.13 = (f32[256]{0:T(256)}, bf16[256,128]{0,1:T(8,128)(2,1)}) all-reduce(f32[256]{0:T(256)S(1)} %scatter_custom_fusion.2, f32[256,128]{0,1:T(8,128)S(1)} %copy.69), channel_id=1, replica_groups=mesh['group'=32,'member'=8] {'member'}, use_global_device_ids=true, to_apply=%region_8.0 | all-reduce | flops 33024 | bytes 198656 | tf_op jit(solution)/shard_map/psum | solution.py:172
  70.5 11.5 %gather_fusion.1 = bf16[3072,128]{1,0:T(8,128)(2,1)} fusion(bf16[768,128]{1,0:T(8,128)(2,1)S(1)} %pad_maximum_fusion.1, s32[3072]{0:T(1024)S(1)} %get-tuple-element.72), kind=kCustom, calls=%fused_computation.1 | custom fusion | bytes 1585152 | tf_op jit(solution)/shard_map/gather | solution.py:119
  82.0 1.4 constant_dynamic-update-slice_fusion.1
  83.6 1.9 multiply_convert_fusion
  85.6 1.3 fusion.98
  87.4 1.3 convert_multiply_fusion.1
  88.8 3.1 copy.57
  91.8 17.3 %scatter_custom_fusion = f32[512,128]{1,0:T(8,128)S(1)} fusion(s32[3072]{0:T(1024)S(1)} %copy-done.51, f32[3072,128]{1,0:T(8,128)} %copy.57, f32[]{:T(128)} %constant.16.clone.1), kind=kCustom, calls=%fused_computation.120 | custom fusion | flops 393216 | bytes 262656 | tf_op jit(solution)/shard_map/scatter-add | solution.py:38
  111.8 2.4 scatter_custom_fusion.1
  116.1 65.6 %all-reduce.8.cloned.1.call-done = f32[256,128]{0,1:T(8,128)} async-done(((f32[256,128]{0,1:T(8,128)}), f32[256,128]{0,1:T(8,128)}) %all-reduce.8.cloned.1.call-update) | async-done | bytes 131088 | tf_op jit(solution)/shard_map/psum | solution.py:172
  185.0 3.1 collective-permute-start.2
  188.1 1.3 collective-permute-start.3
  189.4 1.3 pad_clamp_fusion.2
  191.4 2.3 copy.77
  194.9 3.2 gather_fusion.5
  198.3 4.1 gather_fusion.4
  203.6 1.3 multiply_convert_fusion.2
  207.1 2.3 copy.64
  209.4 9.7 %scatter_custom_fusion.3 = f32[256,128]{1,0:T(8,128)} fusion(s32[1536]{0:T(1024)} %param.29, f32[1536,128]{1,0:T(8,128)} %copy.64, f32[]{:T(128)} %constant.16.clone.1), kind=kCustom, calls=%fused_computation.130 | custom fusion | flops 196608 | bytes 131584 | tf_op jit(solution)/shard_map/scatter-add | solution.py:38
  221.6 1.6 fusion.32
  225.7 4.0 gather_fusion.7
  229.7 2.3 copy.71
  232.0 1.4 multiply_reduce_fusion.3
  233.8 1.3 fusion.1
  235.1 1.6 fusion.103
  236.7 9.1 %scatter_custom_fusion.5 = f32[512,128]{1,0:T(8,128)} fusion(s32[1536]{0:T(1024)} %param.28, f32[1536,256]{1,0:T(8,128)} %fusion.103, f32[]{:T(128)} %constant.16.clone.1), kind=kCustom, calls=%fused_computation.59 | custom fusion | flops 196608 | bytes 1049088 | tf_op jit(solution)/shard_map/scatter-add | solution.py:38
  245.8 1.6 fusion.97
  248.2 1.7 fusion.46
  250.8 4.1 collective-permute-start.4
  255.0 1.4 collective-permute-start.5
  256.4 9.4 %scatter_custom_fusion.6 = f32[256,128]{1,0:T(8,128)S(1)} fusion(f32[256,128]{1,0:T(8,128)S(1)} %slice-done.3, s32[1536]{0:T(1024)} %param.29, f32[1536,256]{1,0:T(8,128)} %fusion.103), kind=kCustom, calls=%fused_computation.57 | custom fusion | flops 196608 | bytes 917504 | tf_op jit(solution)/shard_map/scatter-add | solution.py:38
  267.0 1.3 gather_fusion.6
  270.3 1.7 scatter_custom_fusion.7
  277.4 10.9 %gather_fusion.9 = f32[3072,128]{1,0:T(8,128)} fusion(f32[512,128]{1,0:T(8,128)S(1)} %convert_element_type.201, s32[3072]{0:T(1024)S(1)} %copy-done.39), kind=kCustom, calls=%fused_computation.9 | custom fusion | bytes 3158016 | tf_op jit(solution)/shard_map/gather | solution.py:220
  288.2 3.1 copy.78
  291.3 1.8 add_convert_fusion
  296.1 1.7 fusion
  297.8 1.5 fusion.106
  301.0 2.1 fusion.107
  303.9 2.1 copy-done.2
  306.0 16.6 %scatter_custom_fusion.8 = f32[768,128]{1,0:T(8,128)} fusion(s32[3072]{0:T(1024)} %param.22, f32[3072,384]{1,0:T(8,128)} %copy-done.2, f32[]{:T(128)} %constant.16.clone.1), kind=kCustom, calls=%fused_computation.37 | custom fusion | flops 393216 | bytes 1966592 | tf_op jit(solution)/shard_map/scatter-add | solution.py:38
  323.5 1.7 copy.89
  325.2 1.6 fusion.9
  326.8 4.4 collective-permute-start.6
  331.3 2.4 collective-permute-start.7
  334.0 1.2 copy.84
  335.3 17.7 %scatter_custom_fusion.9 = f32[512,128]{1,0:T(8,128)S(1)} fusion(f32[512,128]{1,0:T(8,128)S(1)} %copy.80, s32[3072]{0:T(1024)} %param.23, f32[3072,384]{1,0:T(8,128)} %copy-done.2), kind=kCustom, calls=%fused_computation.35 | custom fusion | flops 393216 | bytes 1835008 | tf_op jit(solution)/shard_map/scatter-add | solution.py:38
  353.0 1.7 scatter_custom_fusion.10
  355.4 204.3 %all-reduce.10.cloned.1.call-done = (f32[384,128]{1,0:T(8,128)}, f32[256,128]{1,0:T(8,128)}, f32[1,128,128]{2,1,0:T(8,128)}, f32[1,128,128]{2,1,0:T(8,128)}, f32[1,128,128]{2,1,0:T(8,128)}) async-done(((f32[384,128]{1,0:T(8,128)}, f32[256,128]{1,0:T(8,128)}, f32[1,128,128]{2,1,0:T(8,128)}, f32[1,128,128]{2,1,0:T(8,128)}, f32[1,128,128]{2,1,0:T(8,128)}), (f32[384,128]{1,0:T(8,128)}, f32[256,128]{1,0:T(8,128)}, ...) | async-done | bytes 524304 | tf_op jit(solution)/shard_map/psum | solution.py:235
  561.4 144.1 %all-reduce.12.cloned.1.call-done = (f32[256,128]{1,0:T(8,128)}, f32[256,128]{1,0:T(8,128)}, f32[1,128,128]{2,1,0:T(8,128)}, f32[1,128,128]{2,1,0:T(8,128)}) async-done(((f32[256,128]{1,0:T(8,128)}, f32[256,128]{1,0:T(8,128)}, f32[1,128,128]{2,1,0:T(8,128)}, f32[1,128,128]{2,1,0:T(8,128)}), (f32[256,128]{1,0:T(8,128)}, f32[256,128]{1,0:T(8,128)}, f32[1,128,128]{2,1,0:T(8,128)}, ...) | async-done | bytes 393232 | tf_op jit(solution)/shard_map/psum | solution.py:239
  708.0 1.7 copy.114
  709.8 1.6 copy.115
  711.3 1.6 copy.116
  712.9 1.6 copy.117
  (254 shorter events, 44.8 us)
Async XLA Ops:
  7.2 76.5 %copy-start = (bf16[384,128]{1,0:T(8,128)(2,1)S(1)}, bf16[384,128]{1,0:T(8,128)(2,1)}, u32[]{:S(2)}) copy-start(bf16[384,128]{1,0:T(8,128)(2,1)} %param.33) | copy-start | bytes 294916
  7.2 12.5 %copy-start.58 = (s32[1,2,128]{2,1,0:T(2,128)S(1)}, s32[1,2,128]{2,1,0:T(2,128)}, u32[]{:S(2)}) copy-start(s32[1,2,128]{2,1,0:T(2,128)} %param.31) | copy-start | bytes 3076
  7.2 13.0 %copy-start.59 = (s32[1,2]{1,0:T(1,128)S(1)}, s32[1,2]{1,0:T(1,128)}, u32[]{:S(2)}) copy-start(s32[1,2]{1,0:T(1,128)} %param.32) | copy-start | bytes 28
  7.2 13.6 %copy-start.53 = (s32[1536]{0:T(1024)S(1)}, s32[1536]{0:T(1024)}, u32[]{:S(2)}) copy-start(s32[1536]{0:T(1024)} %param.28) | copy-start | bytes 18436
  7.2 14.2 %copy-start.54 = (s32[1536]{0:T(1024)S(1)}, s32[1536]{0:T(1024)}, u32[]{:S(2)}) copy-start(s32[1536]{0:T(1024)} %param.29) | copy-start | bytes 18436
  7.2 14.9 %copy-start.57 = (s32[512]{0:T(512)S(1)}, s32[512]{0:T(512)}, u32[]{:S(2)}) copy-start(s32[512]{0:T(512)} %param.27) | copy-start | bytes 6148
  7.2 15.5 %copy-start.50 = (s32[3072]{0:T(1024)S(1)}, s32[3072]{0:T(1024)}, u32[]{:S(2)}) copy-start(s32[3072]{0:T(1024)} %param.22) | copy-start | bytes 36868
  7.3 15.5 %copy-start.51 = (s32[3072]{0:T(1024)S(1)}, s32[3072]{0:T(1024)}, u32[]{:S(2)}) copy-start(s32[3072]{0:T(1024)} %param.23) | copy-start | bytes 36868
  7.3 15.5 %copy-start.16 = (bf16[512,128]{1,0:T(8,128)(2,1)S(1)}, bf16[512,128]{1,0:T(8,128)(2,1)}, u32[]{:S(2)}) copy-start(bf16[512,128]{1,0:T(8,128)(2,1)} %param.38) | copy-start | bytes 393220
  7.3 174.4 %all-reduce.8.cloned.1.call-start = ((), (), s32[]{:S(2)}) async-start(), calls=%async_computation | async-start | bytes 262144 | tf_op jit(solution)/shard_map/psum | solution.py:172
  11.1 59.4 %collective-permute-start = (bf16[128,128]{1,0:T(8,128)(2,1)S(1)}, bf16[128,128]{1,0:T(8,128)(2,1)S(1)}, u32[]{:S(2)}, u32[]{:S(2)}) collective-permute-start(bf16[128,128]{1,0:T(8,128)(2,1)S(1)} %get-tuple-element.54), channel_id=1, source_target_pairs={{0,1},{1,2},{2,3},{3,4},{4,5},{5,6},{6,7},{7,8},{8,9},{9,10},{10,1... | collective-permute-start | bytes 98312 | tf_op jit(solution)/shard_map/ppermute | solution.py:20
  15.7 11.6 %copy-start.1 = (bf16[512,128]{1,0:T(8,128)(2,1)S(1)}, bf16[512,128]{1,0:T(8,128)(2,1)}, u32[]{:S(2)}) copy-start(bf16[512,128]{1,0:T(8,128)(2,1)} %param.20) | copy-start | bytes 393220
  15.7 54.7 %collective-permute-start.1 = (bf16[128,128]{1,0:T(8,128)(2,1)S(1)}, bf16[128,128]{1,0:T(8,128)(2,1)S(1)}, u32[]{:S(2)}, u32[]{:S(2)}) collective-permute-start(bf16[128,128]{1,0:T(8,128)(2,1)S(1)} %get-tuple-element.55), channel_id=1, source_target_pairs={{1,0},{2,1},{3,2},{4,3},{5,4},{6,5},{7,6},{8,7},{9,8},{10,9},{11,1... | collective-permute-start | bytes 98312 | tf_op jit(solution)/shard_map/ppermute | solution.py:22
  21.5 173.4 %copy-start.40 = (s32[2048]{0:T(1024)}, s32[2048]{0:T(1024)S(1)}, u32[]{:S(2)}) copy-start(s32[2048]{0:T(1024)S(1)} %pad_clamp_fusion) | copy-start | bytes 24580
  22.7 16.1 %copy-start.38 = (s32[3072]{0:T(1024)}, s32[3072]{0:T(1024)S(1)}, u32[]{:S(2)}) copy-start(s32[3072]{0:T(1024)S(1)} %get-tuple-element.73) | copy-start | bytes 36868
  82.0 1.4 copy-start.9
  83.6 1.9 copy-start.4
  85.6 1.5 copy-start.6
  85.6 1.5 copy-start.8
  88.8 21.1 %copy-start.30 = (bf16[256,128]{1,0:T(8,128)(2,1)S(1)}, bf16[256,128]{1,0:T(8,128)(2,1)}, u32[]{:S(2)}) copy-start(bf16[256,128]{1,0:T(8,128)(2,1)} %param.34) | copy-start | bytes 196612
  111.7 70.0 %copy-start.18 = (bf16[512,128]{0,1:T(8,128)(2,1)}, bf16[512,128]{0,1:T(8,128)(2,1)S(1)}, u32[]{:S(2)}) copy-start(bf16[512,128]{0,1:T(8,128)(2,1)S(1)} %add_convert_fusion.4) | copy-start | bytes 393220
  115.0 444.7 %all-reduce.10.cloned.1.call-start = ((), (), s32[]{:S(2)}) async-start(), calls=%async_computation.1 | async-start | bytes 1048576 | tf_op jit(solution)/shard_map/psum | solution.py:235
  185.0 13.1 %collective-permute-start.2 = (bf16[128,128]{0,1:T(8,128)(2,1)}, bf16[128,128]{0,1:T(8,128)(2,1)S(1)}, u32[]{:S(2)}, u32[]{:S(2)}) collective-permute-start(bf16[128,128]{0,1:T(8,128)(2,1)} %get-tuple-element.52), channel_id=1, source_target_pairs={{0,8},{8,16},{16,24},{24,32},{32,40},{40,48},{48,56},{56,64},{64,7... | collective-permute-start | bytes 98312 | tf_op jit(solution)/shard_map/ppermute | solution.py:20
  188.1 10.1 %collective-permute-start.3 = (bf16[128,128]{0,1:T(8,128)(2,1)S(1)}, bf16[128,128]{0,1:T(8,128)(2,1)S(1)}, u32[]{:S(2)}, u32[]{:S(2)}) collective-permute-start(bf16[128,128]{0,1:T(8,128)(2,1)S(1)} %get-tuple-element.53), channel_id=1, source_target_pairs={{8,0},{16,8},{24,16},{32,24},{40,32},{48,40},{56,48},{64,56},{72,6... | collective-permute-start | bytes 98312 | tf_op jit(solution)/shard_map/ppermute | solution.py:22
  194.9 3.4 copy-start.47
  206.1 3.4 copy-start.34
  206.1 14.1 %copy-start.28 = (bf16[256,128]{1,0:T(8,128)(2,1)S(1)}, bf16[256,128]{1,0:T(8,128)(2,1)}, u32[]{:S(2)}) copy-start(bf16[256,128]{1,0:T(8,128)(2,1)} %param.36) | copy-start | bytes 196612
  207.1 14.4 %copy-start.21 = (bf16[256,128]{0,1:T(8,128)(2,1)S(1)}, bf16[256,128]{0,1:T(8,128)(2,1)}, u32[]{:S(2)}) copy-start(bf16[256,128]{0,1:T(8,128)(2,1)} %get-tuple-element.45) | copy-start | bytes 196612
  220.4 2.8 copy-start.36
  223.2 2.5 copy-start.43
  229.7 2.3 copy-start.33
  229.7 2.3 copy-start.35
  232.0 1.5 copy-start.3
  232.0 1.7 copy-start.60
  233.7 1.4 copy-start.14
  235.1 12.2 %copy-start.13 = (bf16[1536,128]{1,0:T(8,128)(2,1)}, bf16[1536,128]{1,0:T(8,128)(2,1)S(1)}, u32[]{:S(2)}) copy-start(bf16[1536,128]{1,0:T(8,128)(2,1)S(1)} %fusion.1) | copy-start | bytes 1179652
  236.7 13.3 %copy-start.15 = (bf16[1536,128]{0,1:T(8,128)(2,1)S(1)}, bf16[1536,128]{0,1:T(8,128)(2,1)}, u32[]{:S(2)}) copy-start(bf16[1536,128]{0,1:T(8,128)(2,1)} %copy-done.14) | copy-start | bytes 1179652
  245.7 10.6 %slice-start.3 = ((f32[512,128]{1,0:T(8,128)}), f32[256,128]{1,0:T(8,128)S(1)}, s32[]{:S(2)}) async-start(f32[512,128]{1,0:T(8,128)} %scatter_custom_fusion.5), calls=%async_computation.6 | async-start | bytes 262144 | tf_op jit(solution)/shard_map/slice | solution.py:211
  247.3 19.7 %copy-start.48 = (s32[1024]{0:T(1024)S(1)}, s32[1024]{0:T(1024)}, u32[]{:S(2)}) copy-start(s32[1024]{0:T(1024)} %pad_clamp_fusion.2) | copy-start | bytes 12292
  250.8 17.6 %copy-start.19 = (bf16[512,128]{0,1:T(8,128)(2,1)S(1)}, bf16[512,128]{0,1:T(8,128)(2,1)}, u32[]{:S(2)}) copy-start(bf16[512,128]{0,1:T(8,128)(2,1)} %copy-done.18) | copy-start | bytes 393220
  250.8 19.4 %collective-permute-start.4 = (f32[128,128]{1,0:T(8,128)}, f32[128,128]{1,0:T(8,128)S(1)}, u32[]{:S(2)}, u32[]{:S(2)}) collective-permute-start(f32[128,128]{1,0:T(8,128)} %get-tuple-element.48), channel_id=1, source_target_pairs={{0,8},{8,16},{16,24},{24,32},{32,40},{40,48},{48,56},{56,64},{64,7... | collective-permute-start | bytes 196616 | tf_op jit(solution)/shard_map/ppermute | solution.py:20
  254.9 14.4 %copy-start.17 = (bf16[512,128]{1,0:T(8,128)(2,1)S(1)}, bf16[512,128]{1,0:T(8,128)(2,1)}, u32[]{:S(2)}) copy-start(bf16[512,128]{1,0:T(8,128)(2,1)} %param.38) | copy-start | bytes 393220
  254.9 15.3 %copy-start.56 = (f32[256]{0:T(256)S(1)}, f32[256]{0:T(256)}, u32[]{:S(2)}) copy-start(f32[256]{0:T(256)} %get-tuple-element.58) | copy-start | bytes 3076
  255.0 15.3 %collective-permute-start.5 = (f32[128,128]{1,0:T(8,128)}, f32[128,128]{1,0:T(8,128)S(1)}, u32[]{:S(2)}, u32[]{:S(2)}) collective-permute-start(f32[128,128]{1,0:T(8,128)} %get-tuple-element.49), channel_id=1, source_target_pairs={{8,0},{16,8},{24,16},{32,24},{40,32},{48,40},{56,48},{64,56},{72,6... | collective-permute-start | bytes 196616 | tf_op jit(solution)/shard_map/ppermute | solution.py:22
  265.8 6.2 copy-start.22
  266.1 6.1 copy-start.52
  273.6 2.5 copy-start.24
  274.3 2.8 copy-start.31
  275.1 2.2 copy-start.39
  277.3 10.9 %copy-start.12 = (f32[512,256]{1,0:T(8,128)}, f32[512,256]{1,0:T(8,128)S(1)}, u32[]{:S(2)}) copy-start(f32[512,256]{1,0:T(8,128)S(1)} %fusion.104) | copy-start | bytes 1572868
  294.7 1.4 copy-start.61
  296.1 1.7 copy-start.5
  297.8 1.6 copy-start.37
  297.8 1.6 copy-start.44
  297.8 3.2 copy-start.11
  299.3 406.1 %all-reduce.12.cloned.1.call-start = ((), (), s32[]{:S(2)}) async-start(), calls=%async_computation.2 | async-start | bytes 786432 | tf_op jit(solution)/shard_map/psum | solution.py:239
  303.9 2.1 copy-start.2
  306.0 17.5 %slice-start = ((f32[3072,384]{1,0:T(8,128)}), f32[3072,128]{1,0:T(8,128)S(1)}, s32[]{:S(2)}) async-start(f32[3072,384]{1,0:T(8,128)} %copy-done.2), calls=%async_computation.3 | async-start | bytes 3145728 | tf_op jit(solution)/shard_map/slice | solution.py:224
  325.2 8.5 %slice-start.2 = ((f32[768,128]{1,0:T(8,128)}), f32[512,128]{1,0:T(8,128)S(1)}, s32[]{:S(2)}) async-start(f32[768,128]{1,0:T(8,128)} %scatter_custom_fusion.8), calls=%async_computation.5 | async-start | bytes 524288 | tf_op jit(solution)/shard_map/slice | solution.py:232
  325.2 8.6 %slice-start.1 = ((f32[512,256]{1,0:T(8,128)}), f32[512,128]{1,0:T(8,128)S(1)}, s32[]{:S(2)}) async-start(f32[512,256]{1,0:T(8,128)} %copy-done.12), calls=%async_computation.4 | async-start | bytes 524288 | tf_op jit(solution)/shard_map/slice | solution.py:230
  326.8 26.2 %collective-permute-start.6 = (f32[128,128]{1,0:T(8,128)S(1)}, f32[128,128]{1,0:T(8,128)S(1)}, u32[]{:S(2)}, u32[]{:S(2)}) collective-permute-start(f32[128,128]{1,0:T(8,128)S(1)} %get-tuple-element.46), channel_id=1, source_target_pairs={{0,1},{1,2},{2,3},{3,4},{4,5},{5,6},{6,7},{7,8},{8,9},{9,10},{10,1... | collective-permute-start | bytes 196616 | tf_op jit(solution)/shard_map/ppermute | solution.py:20
  331.3 21.7 %collective-permute-start.7 = (f32[128,128]{1,0:T(8,128)S(1)}, f32[128,128]{1,0:T(8,128)S(1)}, u32[]{:S(2)}, u32[]{:S(2)}) collective-permute-start(f32[128,128]{1,0:T(8,128)S(1)} %get-tuple-element.47), channel_id=1, source_target_pairs={{1,0},{2,1},{3,2},{4,3},{5,4},{6,5},{7,6},{8,7},{9,8},{10,9},{11,1... | collective-permute-start | bytes 196616 | tf_op jit(solution)/shard_map/ppermute | solution.py:22
  335.2 17.9 %copy-start.55 = (f32[256]{0:T(256)S(1)}, f32[256]{0:T(256)}, u32[]{:S(2)}) copy-start(f32[256]{0:T(256)} %get-tuple-element.56) | copy-start | bytes 3076
  708.0 6.4 copy-start.49
  (13 other events, 13.3 us)
Sparse Core Ops, SparseCore 0:
  115.1 66.5 all-reduce.7
  299.5 260.2 all-reduce.9
  565.0 140.3 all-reduce.11
where the time goes:
time: 736 us; the launch traced here: 721 us
  waiting for transfers between devices  414 us (56%)
  other arithmetic  113 us (15%)
  local copies, waits for them, and re-layouts  100 us (14%)
  matrix products  29 us (4%)
  blocking collectives  24.7 us (3%)
  starting transfers between devices  23.9 us (3%)
  between operations  16.6 us (2%)
    psum x1, waiting for transfers between devices, on_device(): lax.psum((grad_edge_first, grad_edge_second, grad_node_first, grad_node_s...  204 us
    psum x1, waiting for transfers between devices, on_device(): lax.psum((grad_cedge_first, grad_cedge_second, grad_cnode_first, grad_cno...  144 us
    scatter-add x11, other arithmetic, segment_total(): return jax.ops.segment_sum(values, indices, num_segments=row_count)  92.4 us
    psum x1, waiting for transfers between devices, on_device(): pooled_sums, divisor = lax.psum((local_sums, local_counts), 'member')  65.6 us
    unnamed x146, local copies, waits for them, and re-layouts  30.6 us
    psum x1, blocking collectives, on_device(): pooled_sums, divisor = lax.psum((local_sums, local_counts), 'member')  24.7 us
    ppermute x4, starting transfers between devices, with_halo(): lax.ppermute(tail, axis, [(i, (i + 1) % count) for i in range(ends)])  16.2 us
  transfers between devices with their start and end apart: 11, of which 3 were waited for; matrix products, arithmetic and copies ran while one was open for 14% of the time, Pallas kernels for 0%

commit v1 on v0

v1 whole, which is shorter than its diff:
```python
import functools

import jax
import jax.numpy as jnp
from jax import lax
from jax.experimental import pallas as pl
from jax.experimental.pallas import tpu as pltpu
from jax.sharding import Mesh
from jax.sharding import PartitionSpec as P

F32 = jnp.float32
BF = jnp.bfloat16
I32 = jnp.int32
EPS = 1e-05

L = 128
NF = 512
EF = 3072
NC = 256
EC = 1536
SLOT = 128
BLK = 4
CNT = 16
GRADS = 1792
ROWS_EDGE, ROWS_NODE, ROWS_CEDGE, ROWS_CNODE, ROWS_OUTS = 0, 384, 640, 896, 1152

EVERY = ("z", "x", "y", "c")
GROUP = ("z", "x")
PLANE = ("x", "y", "c")

VMEM = pl.BlockSpec(memory_space=pltpu.VMEM)
SMEM = pl.BlockSpec(memory_space=pltpu.SMEM)


def call(kernel, name, out_shape, ins, specs, flops=10**9):
    size = sum(a.size * a.dtype.itemsize for a in ins)
    return pl.pallas_call(
        kernel,
        name=name,
        out_shape=out_shape,
        in_specs=specs,
        out_specs=jax.tree.map(lambda _: VMEM, out_shape),
        cost_estimate=pl.CostEstimate(flops=flops, bytes_accessed=size, transcendentals=0),
        compiler_params=pltpu.CompilerParams(vmem_limit_bytes=48 * 2**20),
    )(*ins)


def shape(*dims, dtype=BF):
    return jax.ShapeDtypeStruct(dims, dtype)


def dot(a, b):
    return jnp.dot(a, b, preferred_element_type=F32)


def dot_nt(a, b):
    return lax.dot_general(a, b, (((1,), (1,)), ((), ())), preferred_element_type=F32)


def dot_tn(a, b):
    return lax.dot_general(a, b, (((0,), (0,)), ((), ())), preferred_element_type=F32)


def mean(v):
    return jnp.mean(v, axis=-1, keepdims=True)


def columns(rows):
    pad = -rows.shape[0] % 8
    rows = rows.astype(F32)
    if pad:
        rows = jnp.concatenate([rows, jnp.zeros((pad, 128), F32)], 0)
    return rows.T.astype(I32)


def pick(cols, blocks, n):
    lane = lax.broadcasted_iota(I32, (128, n), 1)
    return jnp.concatenate(
        [jnp.where(lane == cols[:, j : j + 1], 1.0, 0.0).astype(BF) for j in blocks], 0
    )


def put(rows, blocks, n):
    line = lax.broadcasted_iota(I32, (n, 128), 0)
    return jnp.concatenate(
        [jnp.where(line == rows[j : j + 1, :], 1.0, 0.0).astype(BF) for j in blocks], 1
    )


def live_rows(rows, count):
    at = lax.broadcasted_iota(I32, rows.shape, 0) * 128 + lax.broadcasted_iota(I32, rows.shape, 1)
    return jnp.where(at < count, rows, -1)


def live_slots(send, counts):
    lane = lax.broadcasted_iota(I32, (1, SLOT), 1)
    return jnp.concatenate(
        [jnp.where(lane < counts[0, s], send[s : s + 1, :], -1) for s in (0, 1)], 0
    )


def sigmoid(a):
    return 1.0 / (1.0 + jnp.exp(-a))


def normed_of(hidden, w_second):
    outcome = dot(hidden, w_second)
    centred = outcome - mean(outcome)
    inv = lax.rsqrt(mean(centred * centred) + EPS)
    return centred * inv, inv


def forward(a, w_second):
    hidden = (a * sigmoid(a)).astype(BF)
    return normed_of(hidden, w_second)[0]


def backward(grad, a, w_second):
    sig = sigmoid(a)
    hidden = (a * sig).astype(BF)
    normed, inv = normed_of(hidden, w_second)
    go = (inv * (grad - mean(grad) - normed * mean(grad * normed))).astype(BF)
    gu = dot_nt(go, w_second)
    ga = (gu * (sig * (1.0 + a * (1.0 - sig)))).astype(BF)
    return go, hidden, ga


def send_kernel(node, send, counts, to_prev, to_next):
    cols = columns(live_slots(send[...], counts))
    rows = node[...]
    to_prev[...] = dot(pick(cols, (0,), NF), rows).astype(BF)
    to_next[...] = dot(pick(cols, (1,), NF), rows).astype(BF)


def pre_kernel(edge, node, src, dst, w_in, pool, cot, pre, side):
    w = w_in[...]
    rows = node[...]
    table = jnp.concatenate([dot(rows, w[256:384]), dot(rows, w[128:256])], 0).astype(BF)
    src_cols, dst_cols = columns(src[...]), columns(dst[...])
    for c in range(EF // 128 // BLK):
        blocks = range(c * BLK, (c + 1) * BLK)
        at = pl.ds(c * BLK * 128, BLK * 128)
        hot = jnp.concatenate([pick(dst_cols, blocks, NF), pick(src_cols, blocks, NF)], 1)
        pre[at, :] = dot(edge[at, :], w[:128]) + dot(hot, table)
    pool_hot = put(pool[...], range(NF // 128), NC)
    side[0:NC, :] = dot(pool_hot, cot[...]).astype(BF)
    count = dot_nt(jnp.ones((8, NF), BF), pool_hot)
    high = jnp.floor(count * (1.0 / 16.0))
    low = count - 16.0 * high
    at = lax.broadcasted_iota(I32, (CNT, 128), 0)
    lines = jnp.zeros((CNT, 128), F32)
    for k, v in enumerate((high[0:1, :128], high[0:1, 128:], low[0:1, :128], low[0:1, 128:])):
        lines = jnp.where(at == k, v, lines)
    side[NC : NC + CNT, :] = lines.astype(BF)


def fine_kernel(
    live, pre, edge, node, from_prev, from_next, src, dst, w_in, w_node, w_outs, pool, side,
    new_edges, act, agg_out, act_node, refined, payload,
):
    halo = jnp.concatenate([from_prev[...], from_next[...]], 0)
    table = dot(halo, w_in[128:256, :]).astype(BF)
    src_cols = columns(src[...] - NF)
    dst_rows = live_rows(dst[...], live[0])
    w_second = w_outs[0]
    total = jnp.zeros((NF, L), F32)
    for c in range(EF // 128 // BLK):
        blocks = range(c * BLK, (c + 1) * BLK)
        at = pl.ds(c * BLK * 128, BLK * 128)
        a = pre[at, :] + dot(pick(src_cols, blocks, 2 * SLOT), table)
        act[at, :] = a
        message = forward(a, w_second)
        here = lax.broadcasted_iota(I32, message.shape, 0) + c * BLK * 128 < live[0]
        rows = (edge[at, :].astype(F32) + jnp.where(here, message, 0.0)).astype(BF)
        new_edges[at, :] = rows
        total += dot(put(dst_rows, blocks, NF), rows)
    agg = total.astype(BF)
    agg_out[...] = agg
    a = dot(node[...], w_node[:128, :]) + dot(agg, w_node[128:, :])
    act_node[...] = a
    rows = (node[...].astype(F32) + forward(a, w_outs[1])).astype(BF)
    refined[...] = rows
    payload[0:NC, :] = dot(put(pool[...], range(NF // 128), NC), rows).astype(BF)
    payload[NC:, :] = side[...]


def pair_kernel(pair, out):
    total = (pair[0].astype(F32) + pair[1].astype(F32)).astype(BF)
    for k in range(out.shape[0]):
        out[k] = total


def pool_kernel(parts, send, counts, own_out, cot_out, divisor, to_prev, to_next):
    total = parts[0].astype(F32)
    for k in range(1, parts.shape[0]):
        total += parts[k].astype(F32)
    lines = total[2 * NC :, :]
    count = 16.0 * lines[0:2, :] + lines[2:4, :]
    cols = jnp.concatenate([count, jnp.ones((6, 128), F32)], 0).T
    count = jnp.concatenate(
        [jnp.broadcast_to(cols[:, k : k + 1], (128, L)) for k in (0, 1)], 0
    )
    own = (total[:NC, :] / count).astype(BF)
    own_out[...] = own
    cot_out[...] = total[NC : 2 * NC, :].astype(BF)
    divisor[...] = count
    cols = columns(live_slots(send[...], counts))
    to_prev[...] = dot(pick(cols, (0,), NC), own).astype(BF)
    to_next[...] = dot(pick(cols, (1,), NC), own).astype(BF)


def coarse_pre_kernel(own, cot, src, dst, w_in, w_node, w_outs, pre, pre_node, grad_coarse):
    rows = own[...]
    table = jnp.concatenate([dot(rows, w_in[128:, :]), dot(rows, w_in[:128, :])], 0).astype(BF)
    src_cols, dst_cols = columns(src[...]), columns(dst[...])
    for c in range(EC // 128 // BLK):
        blocks = range(c * BLK, (c + 1) * BLK)
        hot = jnp.concatenate([pick(dst_cols, blocks, NC), pick(src_cols, blocks, NC)], 1)
        pre[pl.ds(c * BLK * 128, BLK * 128), :] = dot(hot, table)
    pre_node[...] = dot(rows, w_node[:128, :])
    grad_coarse[...] = dot_nt(cot[...], w_outs[4]).astype(BF)


def coarse_kernel(
    live, own, pre, pre_node, grad_coarse, from_prev, from_next, src, dst, w_in, w_node, w_outs,
    coarse_out, grad_own, back_prev, back_next, sums_out, seconds, ga_out, agg_out, act,
):
    halo = jnp.concatenate([from_prev[...], from_next[...]], 0)
    table = dot(halo, w_in[:128, :]).astype(BF)
    src_rows = src[...]
    src_cols = columns(src_rows - NC)
    dst_rows = live_rows(dst[...], live[0])
    dst_cols = columns(dst_rows)
    w_second = w_outs[2]
    total = jnp.zeros((NC, L), F32)
    for c in range(EC // 128 // BLK):
        blocks = range(c * BLK, (c + 1) * BLK)
        at = pl.ds(c * BLK * 128, BLK * 128)
        a = pre[at, :] + dot(pick(src_cols, blocks, 2 * SLOT), table)
        act[at, :] = a
        total += dot(put(dst_rows, blocks, NC), forward(a, w_second).astype(BF))
    agg = total.astype(BF)
    agg_out[...] = agg
    a = pre_node[...] + dot(agg, w_node[128:, :])
    rows = own[...]
    coarse_out[...] = (rows.astype(F32) + forward(a, w_outs[3])).astype(BF)
    grad = grad_coarse[...].astype(F32)
    go, hidden, ga = backward(grad, a, w_outs[3])
    ga_out[...] = ga
    seconds[1] = dot_tn(hidden, go)
    grad_total = grad + dot_nt(ga, w_node[:128, :])
    grad_agg = dot_nt(ga, w_node[128:, :]).astype(BF)
    second = jnp.zeros((L, L), F32)
    sums = jnp.zeros((NC + 2 * SLOT + NC, L), F32)
    for c in range(EC // 128 // BLK):
        blocks = range(c * BLK, (c + 1) * BLK)
        at = pl.ds(c * BLK * 128, BLK * 128)
        grad = dot(pick(dst_cols, blocks, NC), grad_agg)
        go, hidden, ga = backward(grad, act[at, :], w_second)
        second += dot_tn(hidden, go)
        hot = jnp.concatenate(
            [put(src_rows, blocks, NC + 2 * SLOT), put(dst_rows, blocks, NC)], 0
        )
        sums += dot(hot, ga)
    seconds[0] = second
    sums = sums.astype(BF)
    sums_out[...] = sums
    grad_ext = dot_nt(sums[: NC + 2 * SLOT], w_in[:128, :])
    grad_own[...] = grad_total + grad_ext[:NC] + dot_nt(sums[NC + 2 * SLOT :], w_in[128:, :])
    back_prev[...] = grad_ext[NC : NC + SLOT].astype(BF)
    back_next[...] = grad_ext[NC + SLOT :].astype(BF)


def lift_kernel(
    own, cot, from_prev, from_next, coarse, sums, seconds, ga, agg, refined, pool, w_outs,
    new_nodes, grads,
):
    part = 1.0 / 8.0
    rows = own[...]
    ext = jnp.concatenate([rows, from_prev[...], from_next[...]], 0)
    both = sums[...]
    lifted = dot(pick(columns(pool[...]), range(NF // 128), NC), coarse[...]).astype(BF)
    new_nodes[...] = (refined[...].astype(F32) + dot(lifted, w_outs[4])).astype(BF)
    grads[0:128, :] = (part * dot_tn(ext, both[: NC + 2 * SLOT])).astype(BF)
    grads[128:256, :] = (part * dot_tn(rows, both[NC + 2 * SLOT :])).astype(BF)
    grads[256:384, :] = (part * dot_tn(rows, ga[...])).astype(BF)
    grads[384:512, :] = (part * dot_tn(agg[...], ga[...])).astype(BF)
    grads[512:640, :] = (part * seconds[0]).astype(BF)
    grads[640:768, :] = (part * seconds[1]).astype(BF)
    grads[768:896, :] = (part * dot_tn(coarse[...], cot[...])).astype(BF)


def fine_back_kernel(
    live, counts, grad_own, divisor, ret_prev, ret_next, send, cot, pool, node, from_prev,
    from_next, act_node, agg, act, edge, cot_edges, src, dst, w_in, w_node, w_outs, coarse_grads,
    grad_edges, grad_node, back_prev, back_next, grads,
):
    back = jnp.concatenate([ret_prev[...], ret_next[...]], 0)
    hot = put(live_slots(send[...], counts), (0, 1), NC)
    grad_pool = (grad_own[...] + dot(hot, back)).astype(BF).astype(F32) / divisor[...]
    pooled = dot(pick(columns(pool[...]), range(NF // 128), NC), grad_pool.astype(BF))
    grad_refined = (cot[...].astype(F32) + pooled).astype(BF).astype(F32)
    go, hidden, ga = backward(grad_refined, act_node[...], w_outs[1])
    rows = node[...]
    node_first = (dot_tn(rows, ga), dot_tn(agg[...], ga))
    node_second = dot_tn(hidden, go)
    grad_total = grad_refined + dot_nt(ga, w_node[:128, :])
    grad_agg = dot_nt(ga, w_node[128:, :]).astype(BF)
    src_rows = src[...]
    dst_rows = live_rows(dst[...], live[0])
    dst_cols = columns(dst_rows)
    w_second = w_outs[0]
    first = jnp.zeros((L, L), F32)
    second = jnp.zeros((L, L), F32)
    sums = jnp.zeros((NF + 2 * SLOT + NF, L), F32)
    for c in range(EF // 128 // BLK):
        blocks = range(c * BLK, (c + 1) * BLK)
        at = pl.ds(c * BLK * 128, BLK * 128)
        gathered = dot(pick(dst_cols, blocks, NF), grad_agg)
        grad_new = (cot_edges[at, :].astype(F32) + gathered).astype(BF).astype(F32)
        here = lax.broadcasted_iota(I32, grad_new.shape, 0) + c * BLK * 128 < live[0]
        go, hidden, ga = backward(jnp.where(here, grad_new, 0.0), act[at, :], w_second)
        grad_edges[at, :] = (grad_new + dot_nt(ga, w_in[:128, :])).astype(BF)
        first += dot_tn(edge[at, :], ga)
        second += dot_tn(hidden, go)
        hot = jnp.concatenate(
            [put(src_rows, blocks, NF + 2 * SLOT), put(dst_rows, blocks, NF)], 0
        )
        sums += dot(hot, ga)
    sums = sums.astype(BF)
    grad_ext = dot_nt(sums[: NF + 2 * SLOT], w_in[128:256, :])
    grad_node[...] = grad_total + grad_ext[:NF] + dot_nt(sums[NF + 2 * SLOT :], w_in[256:, :])
    back_prev[...] = grad_ext[NF : NF + SLOT].astype(BF)
    back_next[...] = grad_ext[NF + SLOT :].astype(BF)
    ext = jnp.concatenate([rows, from_prev[...], from_next[...]], 0)
    grads[0:128, :] = first.astype(BF)
    grads[128:256, :] = dot_tn(ext, sums[: NF + 2 * SLOT]).astype(BF)
    grads[256:384, :] = dot_tn(rows, sums[NF + 2 * SLOT :]).astype(BF)
    grads[384:512, :] = node_first[0].astype(BF)
    grads[512:640, :] = node_first[1].astype(BF)
    grads[640:1152, :] = coarse_grads[0:512, :]
    grads[1152:1280, :] = second.astype(BF)
    grads[1280:1408, :] = node_second.astype(BF)
    grads[1408:1792, :] = coarse_grads[512:896, :]


def node_end_kernel(counts, grad_node, ret_prev, ret_next, send, out):
    back = jnp.concatenate([ret_prev[...], ret_next[...]], 0)
    hot = put(live_slots(send[...], counts), (0, 1), NF)
    out[...] = (grad_node[...] + dot(hot, back)).astype(BF)


def spread_kernel(parts, out):
    total = parts[0].astype(F32)
    for k in range(1, parts.shape[0]):
        total += parts[k].astype(F32)
    total = total.astype(BF)
    for k in range(out.shape[0]):
        out[k] = total


def end_kernel(rows, edge_in, node_in, cedge_in, cnode_in, outs):
    edge_in[...] = rows[ROWS_EDGE:ROWS_NODE, :].astype(F32)
    node_in[...] = rows[ROWS_NODE:ROWS_CEDGE, :].astype(F32)
    cedge_in[...] = rows[ROWS_CEDGE:ROWS_CNODE, :].astype(F32)
    cnode_in[...] = rows[ROWS_CNODE:ROWS_OUTS, :].astype(F32)
    for k in range(5):
        outs[k] = rows[ROWS_OUTS + k * 128 : ROWS_OUTS + (k + 1) * 128, :].astype(F32)


def shift(value, axes, step):
    count = lax.axis_size(axes)
    return lax.ppermute(
        value, axes, [(i, i + step) for i in range(count) if 0 <= i + step < count]
    )


def exchange(value, axes):
    return lax.all_to_all(value, axes, 0, 0)


def on_device(
    node, edge, src, dst, live, send, counts, pool, csrc, cdst, clive, csend, ccounts,
    w_edge, w_node, w_cedge, w_cnode, w_outs, cot, cot_edges,
):
    f32 = functools.partial(shape, dtype=F32)
    slots = (shape(SLOT, L), shape(SLOT, L))
    src, dst = src.reshape(EF // 128, 128), dst.reshape(EF // 128, 128)
    csrc, cdst = csrc.reshape(EC // 128, 128), cdst.reshape(EC // 128, 128)
    pool = pool.reshape(NF // 128, 128)
    send, csend = send.reshape(2, SLOT), csend.reshape(2, SLOT)

    to_prev, to_next = call(
        send_kernel, "send", slots, (node, send, counts), [VMEM, VMEM, SMEM], 10**7
    )
    from_prev, from_next = shift(to_next, EVERY, 1), shift(to_prev, EVERY, -1)
    pre, side = call(
        pre_kernel, "pre", (f32(EF, L), shape(NC + CNT, L)),
        (edge, node, src, dst, w_edge, pool, cot), [VMEM] * 7,
    )
    new_edges, act, agg, act_node, refined, payload = call(
        fine_kernel, "fine",
        (shape(EF, L), f32(EF, L), shape(NF, L), f32(NF, L), shape(NF, L), shape(2 * NC + CNT, L)),
        (live, pre, edge, node, from_prev, from_next, src, dst, w_edge, w_node, w_outs, pool, side),
        [SMEM] + [VMEM] * 12,
    )
    pair = lax.all_gather(payload, "c", axis=0, tiled=False)
    spread = call(pair_kernel, "pair", shape(4, 2 * NC + CNT, L), (pair,), [VMEM], 10**6)
    parts = exchange(spread, "y")
    own, pooled_cot, divisor, to_prev, to_next = call(
        pool_kernel, "pool", (shape(NC, L), shape(NC, L), f32(NC, L)) + slots,
        (parts, csend, ccounts), [VMEM, VMEM, SMEM], 10**7,
    )
    cfrom_prev, cfrom_next = shift(to_next, GROUP, 1), shift(to_prev, GROUP, -1)
    cpre, cpre_node, grad_coarse = call(
        coarse_pre_kernel, "coarse_pre", (f32(EC, L), f32(NC, L), shape(NC, L)),
        (own, pooled_cot, csrc, cdst, w_cedge, w_cnode, w_outs), [VMEM] * 7,
    )
    coarse, grad_own, back_prev, back_next, sums, seconds, cga, cagg, _ = call(
        coarse_kernel, "coarse",
        (shape(NC, L), f32(NC, L)) + slots
        + (shape(2 * NC + 2 * SLOT, L), f32(2, L, L), shape(NC, L), shape(NC, L), f32(EC, L)),
        (clive, own, cpre, cpre_node, grad_coarse, cfrom_prev, cfrom_next, csrc, cdst,
         w_cedge, w_cnode, w_outs),
        [SMEM] + [VMEM] * 11,
    )
    cret_prev, cret_next = shift(back_next, GROUP, 1), shift(back_prev, GROUP, -1)
    new_nodes, coarse_grads = call(
        lift_kernel, "lift", (shape(NF, L), shape(896, L)),
        (own, pooled_cot, cfrom_prev, cfrom_next, coarse, sums, seconds, cga, cagg, refined, pool,
         w_outs),
        [VMEM] * 12,
    )
    grad_edges, grad_node, back_prev, back_next, grads = call(
        fine_back_kernel, "fine_back",
        (shape(EF, L), f32(NF, L)) + slots + (shape(GRADS, L),),
        (live, ccounts, grad_own, divisor, cret_prev, cret_next, csend, cot, pool, node,
         from_prev, from_next, act_node, agg, act, edge, cot_edges, src, dst, w_edge, w_node,
         w_outs, coarse_grads),
        [SMEM, SMEM] + [VMEM] * 21,
    )
    ret_prev, ret_next = shift(back_next, EVERY, 1), shift(back_prev, EVERY, -1)
    parts = exchange(grads.reshape(32, GRADS // 32, L), PLANE)
    spread = call(spread_kernel, "sum_plane", shape(8, GRADS // 32, L), (parts,), [VMEM], 10**6)
    parts = exchange(spread, "z")
    spread = call(spread_kernel, "sum_z", shape(32, GRADS // 32, L), (parts,), [VMEM], 10**6)
    grad_nodes = call(
        node_end_kernel, "node_end", shape(NF, L),
        (counts, grad_node, ret_prev, ret_next, send), [SMEM] + [VMEM] * 4, 10**7,
    )
    rows = exchange(spread, PLANE).reshape(GRADS, L)
    weights = call(
        end_kernel, "end",
        (f32(384, L), f32(256, L), f32(256, L), f32(256, L), f32(5, L, L)),
        (rows,), [VMEM], 10**6,
    )
    return (new_nodes, new_edges, grad_nodes, grad_edges) + tuple(weights)


def solution(mesh):
    cube = Mesh(mesh.devices.reshape(8, 4, 4, 2), EVERY)
    fine, coarse = P(EVERY), P(GROUP)
    in_specs = (fine,) * 8 + (coarse,) * 5 + (P(),) * 5 + (fine,) * 2
    out_specs = (fine,) * 4 + (P(),) * 5
    return jax.shard_map(
        on_device, mesh=cube, in_specs=in_specs, out_specs=out_specs, check_vma=False
    )
```

time: 736 us -> 137 us (0.19); the launches traced: 721 us -> 135 us
  waiting for transfers between devices: 414 us -> 18.4 us
  other arithmetic: 113 us -> 0 us
  local copies, waits for them, and re-layouts: 100 us -> 8.25 us
  Pallas kernels: 0 us -> 29.6 us
  matrix products: 29 us -> 0 us
  blocking collectives: 24.7 us -> 44 us
  between operations: 16.6 us -> 2.31 us
  starting transfers between devices: 23.9 us -> 32.1 us
    psum x3 -> x0, waiting for transfers between devices: 414 us -> none  [the longest x1 204 us: on_device(): lax.psum((grad_edge_first, grad_edge_second, grad_node_first, grad_node_s...]
    scatter-add x11 -> x0, other arithmetic: 92.4 us -> none  [segment_total(): return jax.ops.segment_sum(values, indices, num_segments=row_count)]
    gather x14 -> x0, local copies, waits for them, and re-layouts: 55.6 us -> none  [the longest x2 13.9 us: on_device(): grad_aggregate[edge_dst]]
    all_to_all x0 -> x2, blocking collectives: none -> 41.9 us  [exchange(): return lax.all_to_all(value, axes, 0, 0)]
    pallas_call x0 -> x13, Pallas kernels: none -> 29.6 us  [call(): pl.pallas_call(kernel, name=name, out_shape=out_shape, in_specs=specs, ou...]
    dot_general x27 -> x0, matrix products: 29 us -> none  [the longest x4 6.14 us: mlp_backward(): grad_first = jnp.dot(inputs.T, grad_pre, preferred_element_type=jnp.float32)]
    psum x1 -> x0, blocking collectives: 24.7 us -> none  [on_device(): pooled_sums, divisor = lax.psum((local_sums, local_counts), 'member')]
    unnamed x146 -> x56, local copies, waits for them, and re-layouts: 30.6 us -> 8.25 us
  transfers between devices with their start and end apart: 11 -> 10, of which waited for: 3 -> 5; matrix products, arithmetic and copies ran while one was open for 14% -> 0% of each run, Pallas kernels for 0% -> 4%
where the time goes in v1:
time: 137 us; the launch traced here: 135 us
  blocking collectives  44 us (32%)
  starting transfers between devices  32.1 us (23%)
  Pallas kernels  29.6 us (22%)
  waiting for transfers between devices  18.4 us (13%)
  local copies, waits for them, and re-layouts  8.25 us (6%)
  between operations  2.31 us (2%)
    all_to_all x2, blocking collectives, exchange(): return lax.all_to_all(value, axes, 0, 0)  41.9 us
    pallas_call x13, Pallas kernels, call(): pl.pallas_call(kernel, name=name, out_shape=out_shape, in_specs=specs, ou...  29.6 us
    ppermute x8, starting transfers between devices, shift(): lax.ppermute(value, axes, [(i, i + step) for i in range(count) if 0 <= i...  22.9 us
    ppermute x8, waiting for transfers between devices, shift(): lax.ppermute(value, axes, [(i, i + step) for i in range(count) if 0 <= i...  9.72 us
    all_to_all x2, starting transfers between devices, exchange(): return lax.all_to_all(value, axes, 0, 0)  9.24 us
    all_to_all x2, waiting for transfers between devices, exchange(): return lax.all_to_all(value, axes, 0, 0)  8.65 us
    unnamed x56, local copies, waits for them, and re-layouts  8.25 us
  transfers between devices with their start and end apart: 10, of which 5 were waited for; matrix products, arithmetic and copies ran while one was open for 0% of the time, Pallas kernels for 4%

profile of v1, /device:TPU:1, one launch (start us, length us, event | category | flops | bytes accessed | tf_op | source)
XLA Modules:
  0.0 134.7 jit_solution(11920634906718388603)
XLA Ops:
  0.6 0.0 copy-start.3
  0.7 0.9 copy-done.3
  1.6 0.7 copy-done.16
  2.2 0.7 copy-done.21
  2.9 0.9 send.1
  3.8 4.6 %collective-permute-start = (bf16[128,128]{1,0:T(8,128)(2,1)S(1)}, bf16[128,128]{1,0:T(8,128)(2,1)S(1)}, u32[]{:S(2)}, u32[]{:S(2)}) collective-permute-start(bf16[128,128]{1,0:T(8,128)(2,1)S(1)} %get-tuple-element.48), channel_id=1, source_target_pairs={{0,1},{1,2},{2,3},{3,4},{4,5},{5,6},{6,7},{7,8},{8,9},{9,10},{10,1... | collective-permute-start | bytes 98312 | tf_op jit(solution)/shard_map/ppermute | solution.py:373
  8.4 1.9 %collective-permute-start.1 = (bf16[128,128]{1,0:T(8,128)(2,1)S(1)}, bf16[128,128]{1,0:T(8,128)(2,1)S(1)}, u32[]{:S(2)}, u32[]{:S(2)}) collective-permute-start(bf16[128,128]{1,0:T(8,128)(2,1)S(1)} %get-tuple-element.49), channel_id=1, source_target_pairs={{1,0},{2,1},{3,2},{4,3},{5,4},{6,5},{7,6},{8,7},{9,8},{10,9},{11,1... | collective-permute-start | bytes 98312 | tf_op jit(solution)/shard_map/ppermute | solution.py:373
  10.3 0.0 copy-start
  10.3 1.1 copy-done
  11.5 0.9 copy-done.4
  12.4 0.9 copy-done.7
  13.3 0.9 copy-done.9
  14.2 0.7 copy-done.12
  14.9 0.7 copy-done.14
  15.6 0.7 copy-done.19
  16.3 2.3 %pre.1 = (f32[3072,128]{1,0:T(8,128)S(1)}, bf16[272,128]{1,0:T(8,128)(2,1)S(1)}) custom-call(bf16[3072,128]{1,0:T(8,128)(2,1)S(1)} %copy-done, bf16[512,128]{1,0:T(8,128)(2,1)S(1)} %copy-done.4, s32[24,128]{1,0:T(8,128)S(1)} %bitcast.13, s32[24,128]{1,0:T(8,128)S(1)} %bitcast.16, bf16[384,128]{1,0:T(8,128)(2,1)S(1)} %copy-done.9, s32[4,128]{1,0:T(4,128)S(1)} %bitcast.23, ...), custom_call_target="tpu_custom_call" | custom-call | flops 1000000000 | bytes 1173504 | tf_op jit(solution)/shard_map/pre/pallas_call | solution.py:37
  19.2 0.0 collective-permute-done.from_prev
  19.3 0.0 collective-permute-done.1.from_next
  19.3 0.0 copy-done.6
  19.3 0.0 copy-done.11
  19.3 4.1 %fine.1 = (bf16[3072,128]{1,0:T(8,128)(2,1)}, f32[3072,128]{1,0:T(8,128)S(1)}, bf16[512,128]{1,0:T(8,128)(2,1)S(1)}, f32[512,128]{1,0:T(8,128)S(1)}, bf16[512,12...) custom-call(s32[1]{0:T(128)S(6)} %copy.29.live, f32[3072,128]{1,0:T(8,128)S(1)} %get-tuple-element.47.pre, ...), custom_call_target="tpu_custom_call" | custom-call | flops 1000000000 | bytes 2979844 | tf_op jit(solution)/shard_map/fine/pallas_call | solution.py:37
  23.4 0.0 copy-start.23
  23.4 0.0 copy-start.24
  23.5 0.0 copy-start.25
  23.5 0.0 copy-start.26
  23.5 0.0 copy-start.27
  23.5 2.1 %all-gather = bf16[1056,128]{1,0:T(8,128)(2,1)S(1)} all-gather(bf16[528,128]{1,0:T(8,128)(2,1)S(1)} %get-tuple-element.51), channel_id=2, replica_groups=mesh['z'=8,'x'=4,'y'=4,'c'=2] {'c'}, dimensions={0}, use_global_device_ids=true | all-gather | bytes 405504 | tf_op jit(solution)/shard_map/all_gather | solution.py:407
  25.6 0.8 pair.1
  26.5 4.4 %all-to-all-start = ((bf16[4,528,128]{2,1,0:T(8,128)(2,1)}), bf16[4,528,128]{2,1,0:T(8,128)(2,1)S(1)}, u32[]{:S(2)}, u32[]{:S(2)}) async-start(bf16[4,528,128]{2,1,0:T(8,128)(2,1)} %pair.1), calls=%async_computation | async-start | bytes 1081344 | tf_op jit(solution)/shard_map/all_to_all | solution.py:379
  31.5 8.4 %all-to-all-done.parts = bf16[4,528,128]{2,1,0:T(8,128)(2,1)S(1)} async-done(((bf16[4,528,128]{2,1,0:T(8,128)(2,1)}), bf16[4,528,128]{2,1,0:T(8,128)(2,1)S(1)}, u32[]{:S(2)}, u32[]{:S(2)}) %all-to-all-start) | async-done | bytes 540704 | tf_op jit(solution)/shard_map/all_to_all | solution.py:379
  39.9 0.0 copy-done.23
  39.9 0.9 pool.1
  40.9 4.8 %collective-permute-start.2 = (bf16[128,128]{1,0:T(8,128)(2,1)S(1)}, bf16[128,128]{1,0:T(8,128)(2,1)S(1)}, u32[]{:S(2)}, u32[]{:S(2)}) collective-permute-start(bf16[128,128]{1,0:T(8,128)(2,1)S(1)} %get-tuple-element.54), channel_id=1, source_target_pairs={{0,8},{8,16},{16,24},{24,32},{32,40},{40,48},{48,56},{56,64},{64,7... | collective-permute-start | bytes 98312 | tf_op jit(solution)/shard_map/ppermute | solution.py:373
  45.7 1.5 %collective-permute-start.3 = (bf16[128,128]{1,0:T(8,128)(2,1)S(1)}, bf16[128,128]{1,0:T(8,128)(2,1)S(1)}, u32[]{:S(2)}, u32[]{:S(2)}) collective-permute-start(bf16[128,128]{1,0:T(8,128)(2,1)S(1)} %get-tuple-element.55), channel_id=1, source_target_pairs={{8,0},{16,8},{24,16},{32,24},{40,32},{48,40},{56,48},{64,56},{72,6... | collective-permute-start | bytes 98312 | tf_op jit(solution)/shard_map/ppermute | solution.py:373
  47.2 0.9 coarse_pre.1
  48.1 0.0 collective-permute-done.2.from_prev
  48.1 2.2 %collective-permute-done.3.from_next = bf16[128,128]{1,0:T(8,128)(2,1)S(1)} collective-permute-done((bf16[128,128]{1,0:T(8,128)(2,1)S(1)}, bf16[128,128]{1,0:T(8,128)(2,1)S(1)}, u32[]{:S(2)}, u32[]{:S(2)}) %collective-permute-start.3) | collective-permute-done | bytes 32800 | tf_op jit(solution)/shard_map/ppermute | solution.py:373
  50.3 6.1 %coarse.1 = (bf16[256,128]{1,0:T(8,128)(2,1)S(1)}, f32[256,128]{1,0:T(8,128)S(1)}, bf16[128,128]{1,0:T(8,128)(2,1)S(1)}, bf16[128,128]{1,0:T(8,128)(2,1)S(1)}, b...) custom-call(s32[1]{0:T(128)S(6)} %copy.30.live, ...), custom_call_target="tpu_custom_call" | custom-call | flops 1000000000 | bytes 1421316 | tf_op jit(solution)/shard_map/coarse/pallas_call | solution.py:37
  56.4 3.1 %collective-permute-start.4 = (bf16[128,128]{1,0:T(8,128)(2,1)S(1)}, bf16[128,128]{1,0:T(8,128)(2,1)S(1)}, u32[]{:S(2)}, u32[]{:S(2)}) collective-permute-start(bf16[128,128]{1,0:T(8,128)(2,1)S(1)} %get-tuple-element.69), channel_id=1, source_target_pairs={{0,8},{8,16},{16,24},{24,32},{32,40},{40,48},{48,56},{56,64},{64,7... | collective-permute-start | bytes 98312 | tf_op jit(solution)/shard_map/ppermute | solution.py:373
  59.5 1.5 %collective-permute-start.5 = (bf16[128,128]{1,0:T(8,128)(2,1)S(1)}, bf16[128,128]{1,0:T(8,128)(2,1)S(1)}, u32[]{:S(2)}, u32[]{:S(2)}) collective-permute-start(bf16[128,128]{1,0:T(8,128)(2,1)S(1)} %get-tuple-element.70), channel_id=1, source_target_pairs={{8,0},{16,8},{24,16},{32,24},{40,32},{48,40},{56,48},{64,56},{72,6... | collective-permute-start | bytes 98312 | tf_op jit(solution)/shard_map/ppermute | solution.py:373
  61.0 0.0 copy-start.1
  61.0 0.0 copy-start.2
  61.1 0.0 copy-start.5
  61.1 0.0 copy-start.8
  61.1 0.0 copy-start.10
  61.1 0.0 copy-start.13
  61.1 0.0 copy-start.15
  61.1 1.2 lift.1
  62.3 0.0 collective-permute-done.4.ret_prev
  62.3 3.5 %collective-permute-done.5.ret_next = bf16[128,128]{1,0:T(8,128)(2,1)S(1)} collective-permute-done((bf16[128,128]{1,0:T(8,128)(2,1)S(1)}, bf16[128,128]{1,0:T(8,128)(2,1)S(1)}, u32[]{:S(2)}, u32[]{:S(2)}) %collective-permute-start.5) | collective-permute-done | bytes 32800 | tf_op jit(solution)/shard_map/ppermute | solution.py:373
  65.8 0.0 copy-done.1
  65.9 9.1 %fine_back.1 = (bf16[3072,128]{1,0:T(8,128)(2,1)}, f32[512,128]{1,0:T(8,128)S(1)}, bf16[128,128]{1,0:T(8,128)(2,1)S(1)}, bf16[128,128]{1,0:T(8,128)(2,1)S(1)}, bf16[1792,128]{1,0:T(8,128)(2,1)S(1)}) custom-call(s32[1]{0:T(128)S(6)} %copy.29.live, s32[1,2]{1,0:T(1,128)S(1)} %copy-done.23, f32[256,128]{1,0:T(8,128)S(1)} %get-tuple-element.67.grad_own, ...), custom_call_target="tpu_custom_call" | custom-call | flops 1000000000 | bytes 4779020 | tf_op jit(solution)/shard_map/fine_back/pallas_call | solution.py:37
  75.0 23.3 %all_to_all.20.parts = bf16[32,56,128]{2,1,0:T(8,128)(2,1)S(1)} all-to-all(bf16[32,56,128]{2,1,0:T(8,128)(2,1)S(1)} %bitcast.12), channel_id=1, replica_groups=mesh['z'=8,'x'=4,'y'=4,'c'=2] {'x','y','c'}, dimensions={0} | all-to-all | bytes 917504 | tf_op jit(solution)/shard_map/all_to_all | solution.py:379
  98.3 0.1 sum_plane.1
  98.4 18.6 %all_to_all.21.parts = bf16[8,56,128]{2,1,0:T(8,128)(2,1)S(1)} all-to-all(bf16[8,56,128]{2,1,0:T(8,128)(2,1)S(1)} %sum_plane.1), channel_id=1, replica_groups=mesh['z'=8,'x'=4,'y'=4,'c'=2] {'z'}, dimensions={0} | all-to-all | bytes 229376 | tf_op jit(solution)/shard_map/all_to_all | solution.py:379
  117.0 0.8 sum_z.1
  117.8 4.9 %all-to-all-start.3 = ((bf16[32,56,128]{2,1,0:T(8,128)(2,1)}), bf16[32,56,128]{2,1,0:T(8,128)(2,1)S(1)}, u32[]{:S(2)}, u32[]{:S(2)}) async-start(bf16[32,56,128]{2,1,0:T(8,128)(2,1)} %sum_z.1), calls=%async_computation.3 | async-start | bytes 917504 | tf_op jit(solution)/shard_map/all_to_all | solution.py:379
  122.7 3.5 %collective-permute-start.6 = (bf16[128,128]{1,0:T(8,128)(2,1)S(1)}, bf16[128,128]{1,0:T(8,128)(2,1)S(1)}, u32[]{:S(2)}, u32[]{:S(2)}) collective-permute-start(bf16[128,128]{1,0:T(8,128)(2,1)S(1)} %get-tuple-element.76), channel_id=1, source_target_pairs={{0,1},{1,2},{2,3},{3,4},{4,5},{5,6},{6,7},{7,8},{8,9},{9,10},{10,1... | collective-permute-start | bytes 98312 | tf_op jit(solution)/shard_map/ppermute | solution.py:373
  126.2 1.9 %collective-permute-start.7 = (bf16[128,128]{1,0:T(8,128)(2,1)S(1)}, bf16[128,128]{1,0:T(8,128)(2,1)S(1)}, u32[]{:S(2)}, u32[]{:S(2)}) collective-permute-start(bf16[128,128]{1,0:T(8,128)(2,1)S(1)} %get-tuple-element.77), channel_id=1, source_target_pairs={{1,0},{2,1},{3,2},{4,3},{5,4},{6,5},{7,6},{8,7},{9,8},{10,9},{11,1... | collective-permute-start | bytes 98312 | tf_op jit(solution)/shard_map/ppermute | solution.py:373
  128.1 0.0 collective-permute-done.6.ret_prev
  128.1 3.9 %collective-permute-done.7.ret_next = bf16[128,128]{1,0:T(8,128)(2,1)S(1)} collective-permute-done((bf16[128,128]{1,0:T(8,128)(2,1)S(1)}, bf16[128,128]{1,0:T(8,128)(2,1)S(1)}, u32[]{:S(2)}, u32[]{:S(2)}) %collective-permute-start.7) | collective-permute-done | bytes 32800 | tf_op jit(solution)/shard_map/ppermute | solution.py:373
  132.1 1.4 %node_end.1 = bf16[512,128]{1,0:T(8,128)(2,1)} custom-call(s32[1,2]{1,0:T(1,128)S(1)} %copy-done.22, f32[512,128]{1,0:T(8,128)S(1)} %get-tuple-element.75.grad_node, bf16[128,128]{1,0:T(8,128)(2,1)S(1)} %collective-permute-done.6.ret_prev, bf16[128,128]{1,0:T(8,128)(2,1)S(1)} %collective-permute-done.7.ret_next, s32[2,128]{1,0:T(2,128)S(1)} %bitcast.20), custom_call_target="tpu_custom_call" | custom-call | flops 10000000 | bytes 328712 | tf_op jit(solution)/shard_map/node_end/pallas_call | solution.py:37
  133.5 0.2 all-to-all-done.3
  133.7 1.0 end.1
  (28 shorter events, 0.1 us)
Async XLA Ops:
  0.6 0.9 copy-start.3
  1.5 0.7 copy-start.16
  2.2 0.7 copy-start.21
  3.8 15.5 %collective-permute-start = (bf16[128,128]{1,0:T(8,128)(2,1)S(1)}, bf16[128,128]{1,0:T(8,128)(2,1)S(1)}, u32[]{:S(2)}, u32[]{:S(2)}) collective-permute-start(bf16[128,128]{1,0:T(8,128)(2,1)S(1)} %get-tuple-element.48), channel_id=1, source_target_pairs={{0,1},{1,2},{2,3},{3,4},{4,5},{5,6},{6,7},{7,8},{8,9},{9,10},{10,1... | collective-permute-start | bytes 98312 | tf_op jit(solution)/shard_map/ppermute | solution.py:373
  8.4 10.9 %collective-permute-start.1 = (bf16[128,128]{1,0:T(8,128)(2,1)S(1)}, bf16[128,128]{1,0:T(8,128)(2,1)S(1)}, u32[]{:S(2)}, u32[]{:S(2)}) collective-permute-start(bf16[128,128]{1,0:T(8,128)(2,1)S(1)} %get-tuple-element.49), channel_id=1, source_target_pairs={{1,0},{2,1},{3,2},{4,3},{5,4},{6,5},{7,6},{8,7},{9,8},{10,9},{11,1... | collective-permute-start | bytes 98312 | tf_op jit(solution)/shard_map/ppermute | solution.py:373
  10.3 1.1 copy-start
  11.5 0.9 copy-start.4
  12.4 0.9 copy-start.7
  13.3 0.9 copy-start.9
  14.2 0.7 copy-start.12
  14.9 0.7 copy-start.14
  15.6 0.7 copy-start.19
  16.3 3.0 %copy-start.6 = (bf16[5,128,128]{2,1,0:T(8,128)(2,1)S(1)}, bf16[5,128,128]{2,1,0:T(8,128)(2,1)}, u32[]{:S(2)}) copy-start(bf16[5,128,128]{2,1,0:T(8,128)(2,1)} %w_outs.9) | copy-start | bytes 491524
  16.3 3.0 %copy-start.11 = (bf16[256,128]{1,0:T(8,128)(2,1)S(1)}, bf16[256,128]{1,0:T(8,128)(2,1)}, u32[]{:S(2)}) copy-start(bf16[256,128]{1,0:T(8,128)(2,1)} %w_node.7) | copy-start | bytes 196612
  23.4 16.5 %copy-start.18 = (s32[1,2,128]{2,1,0:T(2,128)S(1)}, s32[1,2,128]{2,1,0:T(2,128)}, u32[]{:S(2)}) copy-start(s32[1,2,128]{2,1,0:T(2,128)} %param.31) | copy-start | bytes 3076
  23.4 16.5 %copy-start.23 = (s32[1,2]{1,0:T(1,128)S(1)}, s32[1,2]{1,0:T(1,128)}, u32[]{:S(2)}) copy-start(s32[1,2]{1,0:T(1,128)} %counts.6) | copy-start | bytes 28
  23.4 23.7 %copy-start.24 = (bf16[256,128]{1,0:T(8,128)(2,1)S(1)}, bf16[256,128]{1,0:T(8,128)(2,1)}, u32[]{:S(2)}) copy-start(bf16[256,128]{1,0:T(8,128)(2,1)} %w_in.8) | copy-start | bytes 196612
  23.5 23.7 %copy-start.25 = (bf16[256,128]{1,0:T(8,128)(2,1)S(1)}, bf16[256,128]{1,0:T(8,128)(2,1)}, u32[]{:S(2)}) copy-start(bf16[256,128]{1,0:T(8,128)(2,1)} %w_node.6) | copy-start | bytes 196612
  23.5 23.7 %copy-start.26 = (s32[1536]{0:T(1024)S(1)}, s32[1536]{0:T(1024)}, u32[]{:S(2)}) copy-start(s32[1536]{0:T(1024)} %param.28) | copy-start | bytes 18436
  23.5 23.7 %copy-start.27 = (s32[1536]{0:T(1024)S(1)}, s32[1536]{0:T(1024)}, u32[]{:S(2)}) copy-start(s32[1536]{0:T(1024)} %param.29) | copy-start | bytes 18436
  26.5 13.5 %all-to-all-start = ((bf16[4,528,128]{2,1,0:T(8,128)(2,1)}), bf16[4,528,128]{2,1,0:T(8,128)(2,1)S(1)}, u32[]{:S(2)}, u32[]{:S(2)}) async-start(bf16[4,528,128]{2,1,0:T(8,128)(2,1)} %pair.1), calls=%async_computation | async-start | bytes 1081344 | tf_op jit(solution)/shard_map/all_to_all | solution.py:379
  40.9 7.2 %collective-permute-start.2 = (bf16[128,128]{1,0:T(8,128)(2,1)S(1)}, bf16[128,128]{1,0:T(8,128)(2,1)S(1)}, u32[]{:S(2)}, u32[]{:S(2)}) collective-permute-start(bf16[128,128]{1,0:T(8,128)(2,1)S(1)} %get-tuple-element.54), channel_id=1, source_target_pairs={{0,8},{8,16},{16,24},{24,32},{32,40},{40,48},{48,56},{56,64},{64,7... | collective-permute-start | bytes 98312 | tf_op jit(solution)/shard_map/ppermute | solution.py:373
  45.7 4.7 %collective-permute-start.3 = (bf16[128,128]{1,0:T(8,128)(2,1)S(1)}, bf16[128,128]{1,0:T(8,128)(2,1)S(1)}, u32[]{:S(2)}, u32[]{:S(2)}) collective-permute-start(bf16[128,128]{1,0:T(8,128)(2,1)S(1)} %get-tuple-element.55), channel_id=1, source_target_pairs={{8,0},{16,8},{24,16},{32,24},{40,32},{48,40},{56,48},{64,56},{72,6... | collective-permute-start | bytes 98312 | tf_op jit(solution)/shard_map/ppermute | solution.py:373
  50.3 10.7 %copy-start.20 = (s32[512]{0:T(512)S(1)}, s32[512]{0:T(512)}, u32[]{:S(2)}) copy-start(s32[512]{0:T(512)} %param.27) | copy-start | bytes 6148
  56.4 5.9 %collective-permute-start.4 = (bf16[128,128]{1,0:T(8,128)(2,1)S(1)}, bf16[128,128]{1,0:T(8,128)(2,1)S(1)}, u32[]{:S(2)}, u32[]{:S(2)}) collective-permute-start(bf16[128,128]{1,0:T(8,128)(2,1)S(1)} %get-tuple-element.69), channel_id=1, source_target_pairs={{0,8},{8,16},{16,24},{24,32},{32,40},{40,48},{48,56},{56,64},{64,7... | collective-permute-start | bytes 98312 | tf_op jit(solution)/shard_map/ppermute | solution.py:373
  59.5 6.3 %collective-permute-start.5 = (bf16[128,128]{1,0:T(8,128)(2,1)S(1)}, bf16[128,128]{1,0:T(8,128)(2,1)S(1)}, u32[]{:S(2)}, u32[]{:S(2)}) collective-permute-start(bf16[128,128]{1,0:T(8,128)(2,1)S(1)} %get-tuple-element.70), channel_id=1, source_target_pairs={{8,0},{16,8},{24,16},{32,24},{40,32},{48,40},{56,48},{64,56},{72,6... | collective-permute-start | bytes 98312 | tf_op jit(solution)/shard_map/ppermute | solution.py:373
  61.0 4.8 %copy-start.1 = (bf16[3072,128]{1,0:T(8,128)(2,1)S(1)}, bf16[3072,128]{1,0:T(8,128)(2,1)}, u32[]{:S(2)}) copy-start(bf16[3072,128]{1,0:T(8,128)(2,1)} %edge.5) | copy-start | bytes 2359300
  61.0 4.8 %copy-start.2 = (bf16[3072,128]{1,0:T(8,128)(2,1)S(1)}, bf16[3072,128]{1,0:T(8,128)(2,1)}, u32[]{:S(2)}) copy-start(bf16[3072,128]{1,0:T(8,128)(2,1)} %cot_edges.1) | copy-start | bytes 2359300
  61.1 4.8 %copy-start.5 = (bf16[512,128]{1,0:T(8,128)(2,1)S(1)}, bf16[512,128]{1,0:T(8,128)(2,1)}, u32[]{:S(2)}) copy-start(bf16[512,128]{1,0:T(8,128)(2,1)} %node.7) | copy-start | bytes 393220
  61.1 4.8 %copy-start.8 = (bf16[512,128]{1,0:T(8,128)(2,1)S(1)}, bf16[512,128]{1,0:T(8,128)(2,1)}, u32[]{:S(2)}) copy-start(bf16[512,128]{1,0:T(8,128)(2,1)} %cot.3) | copy-start | bytes 393220
  61.1 4.8 %copy-start.10 = (bf16[384,128]{1,0:T(8,128)(2,1)S(1)}, bf16[384,128]{1,0:T(8,128)(2,1)}, u32[]{:S(2)}) copy-start(bf16[384,128]{1,0:T(8,128)(2,1)} %w_in.9) | copy-start | bytes 294916
  61.1 4.8 %copy-start.13 = (s32[3072]{0:T(1024)S(1)}, s32[3072]{0:T(1024)}, u32[]{:S(2)}) copy-start(s32[3072]{0:T(1024)} %param.22) | copy-start | bytes 36868
  61.1 4.8 %copy-start.15 = (s32[3072]{0:T(1024)S(1)}, s32[3072]{0:T(1024)}, u32[]{:S(2)}) copy-start(s32[3072]{0:T(1024)} %param.23) | copy-start | bytes 36868
  75.0 57.1 %copy-start.17 = (s32[1,2,128]{2,1,0:T(2,128)S(1)}, s32[1,2,128]{2,1,0:T(2,128)}, u32[]{:S(2)}) copy-start(s32[1,2,128]{2,1,0:T(2,128)} %param.25) | copy-start | bytes 3076
  75.0 57.1 %copy-start.22 = (s32[1,2]{1,0:T(1,128)S(1)}, s32[1,2]{1,0:T(1,128)}, u32[]{:S(2)}) copy-start(s32[1,2]{1,0:T(1,128)} %counts.7) | copy-start | bytes 28
  117.8 16.0 %all-to-all-start.3 = ((bf16[32,56,128]{2,1,0:T(8,128)(2,1)}), bf16[32,56,128]{2,1,0:T(8,128)(2,1)S(1)}, u32[]{:S(2)}, u32[]{:S(2)}) async-start(bf16[32,56,128]{2,1,0:T(8,128)(2,1)} %sum_z.1), calls=%async_computation.3 | async-start | bytes 917504 | tf_op jit(solution)/shard_map/all_to_all | solution.py:379
  122.7 5.5 %collective-permute-start.6 = (bf16[128,128]{1,0:T(8,128)(2,1)S(1)}, bf16[128,128]{1,0:T(8,128)(2,1)S(1)}, u32[]{:S(2)}, u32[]{:S(2)}) collective-permute-start(bf16[128,128]{1,0:T(8,128)(2,1)S(1)} %get-tuple-element.76), channel_id=1, source_target_pairs={{0,1},{1,2},{2,3},{3,4},{4,5},{5,6},{6,7},{7,8},{8,9},{9,10},{10,1... | collective-permute-start | bytes 98312 | tf_op jit(solution)/shard_map/ppermute | solution.py:373
  126.2 5.9 %collective-permute-start.7 = (bf16[128,128]{1,0:T(8,128)(2,1)S(1)}, bf16[128,128]{1,0:T(8,128)(2,1)S(1)}, u32[]{:S(2)}, u32[]{:S(2)}) collective-permute-start(bf16[128,128]{1,0:T(8,128)(2,1)S(1)} %get-tuple-element.77), channel_id=1, source_target_pairs={{1,0},{2,1},{3,2},{4,3},{5,4},{6,5},{7,6},{8,7},{9,8},{10,9},{11,1... | collective-permute-start | bytes 98312 | tf_op jit(solution)/shard_map/ppermute | solution.py:373
